TPU v7x, 1024 devices: a whole 8x8x8 slice. The times are simulated.
1024 devices in a mesh: sec: 128 (over y, z, core), mpo: 8 (over x).
Axes of the slice: x: 8, y: 8, z: 8, core: 2. Of those that a mesh axis runs over, the one named last changes fastest.
Arguments:
- wavefunction: float32 [256, 256, 256], P('sec'), may hold values from -6 to 6
- sector_sizes: int32 [256, 2], P('sec'), may hold values from 128 to 256, as said below
- left_env: float32 [24, 256, 256, 256], P('mpo', 'sec'), may hold values from -0.375 to 0.375
- right_env: float32 [24, 256, 256, 256], P('mpo', 'sec'), may hold values from -0.375 to 0.375
- mpo_coeffs: float32 [24, 256], P('mpo', 'sec'), may hold values from -4 to 4
- source_block: int32 [24, 256], P('mpo', 'sec'), may hold values from 0 to 255, as said below
Outputs:
- applied: float32 [256, 256, 256], P('sec', 'mpo')
Inputs may be any that keep to these rules, and one draw needn't show every extreme that they name: source_block[w, k] lies in the index-of-sec group of block k or in the group just below or just above it, groups being runs of 2 blocks. `sector_sizes`: each entry is a multiple of 128.
All inputs are finite; a program needn't handle non-finite values.
Results may differ from a plain program's by a relative error of at most 0.0001.
Values sent between devices are 32-bit elements; how exact they have to be, the bound alone decides.
No kernel may reach another device: no remote copies, remote signals or barrier semaphores. Data moves between devices by JAX's collectives and lax.ppermute only.
A program may use at most 32 MiB of HBM per device.

v0:
```python
import jax
import jax.numpy as jnp
from jax import lax
from jax.sharding import PartitionSpec as P


def with_halo(value, sides, width):
    for axis, dim in sides:
        devices, length = (lax.axis_size(axis), value.shape[dim])
        up = [(i, (i + 1) % devices) for i in range(devices - 1)]
        down = [(j, i) for i, j in up]
        last = lax.slice_in_dim(value, length - width, length, axis=dim)
        initial = lax.slice_in_dim(value, 0, width, axis=dim)
        before = lax.ppermute(last, axis, up)
        after = lax.ppermute(initial, axis, down)
        value = jnp.concatenate([before, value, after], axis=dim)
    return value


def on_device(wavefunction, sector_sizes, left_env, right_env, mpo_coeffs, source_block):
    block_count = wavefunction.shape[0]
    block_width = wavefunction.shape[1]
    row_index = jnp.arange(block_width, dtype=jnp.int32)
    keep_mask = (row_index[None, :, None] < sector_sizes[:, 0][:, None, None]) & (
        row_index[None, None, :] < sector_sizes[:, 1][:, None, None]
    )
    masked = jnp.where(keep_mask, wavefunction, jnp.zeros_like(wavefunction))
    gathered = with_halo(masked, (("sec", 0),), block_count)
    position = source_block - (lax.axis_index("sec") - 1) * block_count
    chosen = gathered[position] * mpo_coeffs[:, :, None, None]
    left_done = jnp.einsum("wkab,wkbc->wkac", left_env, chosen, precision=lax.Precision.HIGHEST)
    partial_value = jnp.einsum(
        "wkac,wkdc->kad", left_done, right_env, precision=lax.Precision.HIGHEST
    )
    partial_value = jnp.where(keep_mask, partial_value, jnp.zeros_like(partial_value))
    return lax.psum_scatter(partial_value, "mpo", scatter_dimension=1, tiled=True)


def solution(mesh):
    in_specs = (
        P("sec", None, None),
        P("sec", None),
        P("mpo", "sec", None, None),
        P("mpo", "sec", None, None),
        P("mpo", "sec"),
        P("mpo", "sec"),
    )
    out_specs = P("sec", "mpo", None)
    return jax.shard_map(
        on_device, mesh=mesh, in_specs=in_specs, out_specs=out_specs, check_vma=False
    )
```

profile of v0, /device:TPU:112, one launch (start us, length us, event | category | flops | bytes accessed | tf_op | source)
XLA Modules:
  0.0 91.3 jit_solution(6466110324966633601)
XLA Ops:
  6.5 0.0 copy-start
  6.5 0.0 reduce-scatter.2.cloned.1.call-start
  6.5 1.0 %slice_reduce_fusion.1 = (s32[2]{0:T(128)S(1)}, s32[2]{0:T(128)S(1)}) fusion(s32[2,2]{1,0:T(2,128)} %param.7), kind=kLoop, calls=%fused_computation.17 | loop fusion | bytes 32 | tf_op jit(solution)/shard_map/slice | solution.py:24
  7.6 0.1 iota_compare_fusion
  7.6 1.2 %and_select_fusion = f32[2,256,256]{2,1,0:T(8,128)S(1)} fusion(f32[2,256,256]{2,1,0:T(8,128)} %param.6, pred[2,256]{1,0:T(4,128)(4,1)S(1)} %get-tuple-element.7, pred[2,256]{1,0:T(4,128)(4,1)S(1)} %get-tuple-element.8), kind=kLoop, calls=%fused_computation.11 | loop fusion | flops 262144 | bytes 1049600 | tf_op jit(solution)/shard_map/jit(_where)/select_n | solution.py:27
  8.8 0.0 copy-start.1
  8.8 1.9 %collective-permute-start = (f32[2,256,256]{2,1,0:T(8,128)S(1)}, f32[2,256,256]{2,1,0:T(8,128)S(1)}, u32[]{:S(2)}, u32[]{:S(2)}) collective-permute-start(f32[2,256,256]{2,1,0:T(8,128)S(1)} %and_select_fusion), channel_id=1, source_target_pairs={{0,8},{8,16},{16,24},{24,32},{32,40},{40,48},{48,56},{56,64},{64,7... | collective-permute-start | bytes 1572872 | tf_op jit(solution)/shard_map/ppermute | solution.py:14
  10.8 17.4 %collective-permute-start.1 = (f32[2,256,256]{2,1,0:T(8,128)S(1)}, f32[2,256,256]{2,1,0:T(8,128)}, u32[]{:S(2)}, u32[]{:S(2)}) collective-permute-start(f32[2,256,256]{2,1,0:T(8,128)S(1)} %and_select_fusion), channel_id=1, source_target_pairs={{8,0},{16,8},{24,16},{32,24},{40,32},{48,40},{56,48},{64,56},{72,6... | collective-permute-start | bytes 1572872 | tf_op jit(solution)/shard_map/ppermute | solution.py:15
  28.2 0.7 compare_select_fusion
  28.9 0.1 copy.10
  29.0 0.1 reshape.53
  29.1 0.8 copy.11
  29.9 3.3 %collective-permute-done = f32[2,256,256]{2,1,0:T(8,128)S(1)} collective-permute-done((f32[2,256,256]{2,1,0:T(8,128)S(1)}, f32[2,256,256]{2,1,0:T(8,128)S(1)}, u32[]{:S(2)}, u32[]{:S(2)}) %collective-permute-start) | collective-permute-done | bytes 524320 | tf_op jit(solution)/shard_map/ppermute | solution.py:14
  33.1 0.0 copy-done.1
  33.1 0.8 copy-done.3
  33.9 1.0 %collective-permute-done.1 = f32[2,256,256]{2,1,0:T(8,128)} collective-permute-done((f32[2,256,256]{2,1,0:T(8,128)S(1)}, f32[2,256,256]{2,1,0:T(8,128)}, u32[]{:S(2)}, u32[]{:S(2)}) %collective-permute-start.1) | collective-permute-done | bytes 524320 | tf_op jit(solution)/shard_map/ppermute | solution.py:15
  34.9 1.5 %pad_maximum_fusion = f32[6,256,256]{2,1,0:T(8,128)S(1)} fusion(f32[2,256,256]{2,1,0:T(8,128)} %collective-permute-done.1, f32[2,256,256]{2,1,0:T(8,128)} %copy-done.1, f32[2,256,256]{2,1,0:T(8,128)} %copy-done.3), kind=kLoop, calls=%fused_computation.1 | loop fusion | flops 786432 | bytes 3145728 | tf_op jit(solution)/shard_map/concatenate | solution.py:16
  36.3 1.8 %gather_fusion = f32[6,256,256]{2,1,0:T(8,128)} fusion(f32[6,256,256]{2,1,0:T(8,128)S(1)} %pad_maximum_fusion, s32[1024]{0:T(1024)S(1)} %pad_clamp_fusion), kind=kCustom, calls=%fused_computation | custom fusion | bytes 3145752 | tf_op jit(solution)/shard_map/gather | solution.py:30
  38.2 0.0 copy-done
  38.2 3.4 %fusion.2 = f32[3,2,256,256]{2,3,0,1:T(8,128)S(1)} fusion(f32[3,2,256,256]{3,2,1,0:T(8,128)S(1)} %copy-done, f32[3,2,256,256]{3,2,1,0:T(8,128)} %bitcast.13, f32[3,2]{1,0:T(4,128)S(1)} %copy.11), kind=kOutput, calls=%fused_computation.4 | convolution fusion | flops 1208352768 | bytes 4718616 | tf_op jit(solution)/shard_map/wkab,wkbc->wkac/dot_general | solution.py:31
  41.6 0.0 copy-done.2
  41.6 2.4 %fusion.11 = f32[2,256,256]{2,1,0:T(8,128)} fusion(f32[3,2,256,256]{3,2,1,0:T(8,128)S(1)} %copy-done.2, f32[3,2,256,256]{2,3,0,1:T(8,128)S(1)} %fusion.2, pred[2,256]{1,0:T(4,128)(4,1)S(1)} %get-tuple-element.7, pred[2,256]{1,0:T(4,128)(4,1)S(1)} %get-tuple-element.8), kind=kOutput, calls=%fused_computation.9 | convolution fusion | flops 1208221696 | bytes 3671040 | tf_op jit(solution)/shard_map/wkac,wkdc->kad/dot_general | solution.py:32
  44.0 0.0 reduce-scatter.2.cloned.1.call-update
  44.0 40.4 %reduce-scatter.2.cloned.1.call-done = f32[2,32,256]{2,1,0:T(8,128)} async-done(((f32[2,256,256]{2,1,0:T(8,128)}), f32[2,32,256]{2,1,0:T(8,128)}) %reduce-scatter.2.cloned.1.call-update) | async-done | bytes 65552 | tf_op jit(solution)/shard_map/reduce_scatter | solution.py:36
  (3 shorter events, 0.0 us)
Async XLA Ops:
  6.5 31.6 %copy-start = (f32[3,2,256,256]{3,2,1,0:T(8,128)S(1)}, f32[3,2,256,256]{3,2,1,0:T(8,128)}, u32[]{:S(2)}) copy-start(f32[3,2,256,256]{3,2,1,0:T(8,128)} %param.8) | copy-start | bytes 4718596
  6.5 77.9 %reduce-scatter.2.cloned.1.call-start = ((), (), s32[]{:S(2)}) async-start(), calls=%async_computation.1 | async-start | bytes 589824 | tf_op jit(solution)/shard_map/reduce_scatter | solution.py:36
  8.8 24.3 %copy-start.1 = (f32[2,256,256]{2,1,0:T(8,128)}, f32[2,256,256]{2,1,0:T(8,128)S(1)}, u32[]{:S(2)}) copy-start(f32[2,256,256]{2,1,0:T(8,128)S(1)} %and_select_fusion) | copy-start | bytes 1572868
  8.8 24.3 %collective-permute-start = (f32[2,256,256]{2,1,0:T(8,128)S(1)}, f32[2,256,256]{2,1,0:T(8,128)S(1)}, u32[]{:S(2)}, u32[]{:S(2)}) collective-permute-start(f32[2,256,256]{2,1,0:T(8,128)S(1)} %and_select_fusion), channel_id=1, source_target_pairs={{0,8},{8,16},{16,24},{24,32},{32,40},{40,48},{48,56},{56,64},{64,7... | collective-permute-start | bytes 1572872 | tf_op jit(solution)/shard_map/ppermute | solution.py:14
  10.8 24.1 %collective-permute-start.1 = (f32[2,256,256]{2,1,0:T(8,128)S(1)}, f32[2,256,256]{2,1,0:T(8,128)}, u32[]{:S(2)}, u32[]{:S(2)}) collective-permute-start(f32[2,256,256]{2,1,0:T(8,128)S(1)} %and_select_fusion), channel_id=1, source_target_pairs={{8,0},{16,8},{24,16},{32,24},{40,32},{48,40},{56,48},{64,56},{72,6... | collective-permute-start | bytes 1572872 | tf_op jit(solution)/shard_map/ppermute | solution.py:15
  33.1 0.8 copy-start.3
  38.2 3.4 %copy-start.2 = (f32[3,2,256,256]{3,2,1,0:T(8,128)S(1)}, f32[3,2,256,256]{3,2,1,0:T(8,128)}, u32[]{:S(2)}) copy-start(f32[3,2,256,256]{3,2,1,0:T(8,128)} %param.9) | copy-start | bytes 4718596
Sparse Core Ops, SparseCore 0:
  44.1 40.2 reduce-scatter.1
where the time goes:
time: 93.1 us; the launch traced here: 91.3 us
  waiting for transfers between devices  44.6 us (48%)
  starting transfers between devices  19.3 us (21%)
  between operations  13.5 us (15%)
  matrix products  5.81 us (6%)
  local copies, waits for them, and re-layouts  4.6 us (5%)
  other arithmetic  3.41 us (4%)
    reduce_scatter x1, waiting for transfers between devices, on_device(): lax.psum_scatter(partial_value, 'mpo', scatter_dimension=1, tiled=True)  40.4 us
    ppermute x1, starting transfers between devices, with_halo(): after = lax.ppermute(initial, axis, down)  17.4 us
    dot_general x1, matrix products, on_device(): jnp.einsum('wkab,wkbc->wkac', left_env, chosen, precision=lax.Precision.H...  3.39 us
    ppermute x1, waiting for transfers between devices, with_halo(): before = lax.ppermute(last, axis, up)  3.28 us
    dot_general x1, matrix products, on_device(): jnp.einsum('wkac,wkdc->kad', left_done, right_env, precision=lax.Precisio...  2.42 us
    ppermute x1, starting transfers between devices, with_halo(): before = lax.ppermute(last, axis, up)  1.92 us
  transfers between devices with their start and end apart: 3, of which 3 were waited for; matrix products, arithmetic and copies ran while one was open for 2% of the time, Pallas kernels for 0%

commit v1 on v0

v1 whole, which is shorter than its diff:
```python
import functools

import jax
import jax.numpy as jnp
from jax import lax
from jax.experimental import pallas as pl
from jax.experimental.pallas import tpu as pltpu
from jax.sharding import PartitionSpec as P

VMEM_LIMIT = 48 * 1024 * 1024
vmem = pl.BlockSpec(memory_space=pltpu.VMEM)
smem = pl.BlockSpec(memory_space=pltpu.SMEM)


def keep(sizes_ref, k, shape):
    rows = lax.broadcasted_iota(jnp.int32, shape, 0) < sizes_ref[k, 0]
    columns = lax.broadcasted_iota(jnp.int32, shape, 1) < sizes_ref[k, 1]
    return rows & columns


def split(value):
    high = value.astype(jnp.bfloat16)
    return high, (value - high.astype(jnp.float32)).astype(jnp.bfloat16)


def product(left, right, contract):
    dot = functools.partial(
        lax.dot_general,
        dimension_numbers=(((1,), (contract,)), ((), ())),
        preferred_element_type=jnp.float32,
    )
    (left_high, left_low), (right_high, right_low) = left, right
    return dot(left_high, right_high) + (dot(left_high, right_low) + dot(left_low, right_high))


def mask_kernel(sizes_ref, wave_ref, masked_ref):
    blocks, rows, columns = wave_ref.shape
    for k in range(blocks):
        masked_ref[k] = jnp.where(keep(sizes_ref, k, (rows, columns)), wave_ref[k], 0.0)


def near_kernel(
    sizes_ref, coeff_ref, source_ref, own_ref, after_ref, left_ref, right_ref,
    total_ref, left_high, left_low, right_high, right_low,
):
    terms, blocks, rows, columns = left_ref.shape
    parts, _, part, _ = total_ref.shape
    first = lax.axis_index("sec") * blocks
    for k in range(blocks):
        total_ref[:, k] = jnp.zeros((parts, part, columns), jnp.float32)
        for w in range(terms):
            place = source_ref[k, w] - first

            @pl.when(place >= 0)
            def _():
                own = own_ref[jnp.clip(place, 0, blocks - 1)]
                after = after_ref[jnp.clip(place - blocks, 0, blocks - 1)]
                chosen = jnp.where(place < blocks, own, after) * coeff_ref[k, w]
                done = product(split(left_ref[w, k]), split(chosen), 0)
                term = product(split(done), split(right_ref[w, k]), 1)
                term = jnp.where(keep(sizes_ref, k, (rows, columns)), term, 0.0)
                total_ref[:, k] += term.reshape(parts, part, columns)

            @pl.when(place < 0)
            def _():
                high, low = split(left_ref[w, k])
                left_high[w, k] = high
                left_low[w, k] = low
                high, low = split(right_ref[w, k])
                right_high[w, k] = high
                right_low[w, k] = low


def far_kernel(
    sizes_ref, coeff_ref, source_ref, before_ref,
    left_high, left_low, right_high, right_low, sum_ref, total_ref,
):
    terms, blocks, rows, columns = left_high.shape
    parts, _, part, _ = total_ref.shape
    total_ref[...] = sum_ref[...]
    first = lax.axis_index("sec") * blocks
    for k in range(blocks):
        for w in range(terms):
            place = source_ref[k, w] - first

            @pl.when(place < 0)
            def _():
                chosen = before_ref[jnp.clip(place + blocks, 0, blocks - 1)] * coeff_ref[k, w]
                done = product((left_high[w, k], left_low[w, k]), split(chosen), 0)
                term = product(split(done), (right_high[w, k], right_low[w, k]), 1)
                term = jnp.where(keep(sizes_ref, k, (rows, columns)), term, 0.0)
                total_ref[:, k] += term.reshape(parts, part, columns)


def on_device(wavefunction, sector_sizes, left_env, right_env, mpo_coeffs, source_block):
    blocks, rows, columns = wavefunction.shape
    terms = left_env.shape[0]
    devices, parts = lax.axis_size("sec"), lax.axis_size("mpo")
    coeffs, sources = mpo_coeffs.T, source_block.T
    params = pltpu.CompilerParams(vmem_limit_bytes=VMEM_LIMIT)
    f32 = jax.ShapeDtypeStruct((parts, blocks, rows // parts, columns), jnp.float32)
    bf16 = jax.ShapeDtypeStruct((terms, blocks, rows, columns), jnp.bfloat16)

    masked = pl.pallas_call(
        mask_kernel,
        out_shape=jax.ShapeDtypeStruct(wavefunction.shape, jnp.float32),
        in_specs=[smem, vmem],
        out_specs=vmem,
        name="mask",
    )(sector_sizes, wavefunction)

    after = lax.ppermute(masked, "sec", [(i + 1, i) for i in range(devices - 1)])
    before = lax.ppermute(masked, "sec", [(i, i + 1) for i in range(devices - 1)])

    total, *halves = pl.pallas_call(
        near_kernel,
        out_shape=[f32] + [bf16] * 4,
        in_specs=[smem] * 3 + [vmem] * 4,
        out_specs=[vmem] * 5,
        compiler_params=params,
        cost_estimate=pl.CostEstimate(
            flops=12 * 3 * 2 * rows**3, bytes_accessed=8 * 2**20, transcendentals=0
        ),
        name="near_terms",
    )(sector_sizes, coeffs, sources, masked, after, left_env, right_env)

    total = pl.pallas_call(
        far_kernel,
        out_shape=f32,
        in_specs=[smem] * 3 + [vmem] * 6,
        out_specs=vmem,
        compiler_params=params,
        cost_estimate=pl.CostEstimate(
            flops=4 * 3 * 2 * rows**3, bytes_accessed=4 * 2**20, transcendentals=0
        ),
        name="far_terms",
    )(sector_sizes, coeffs, sources, before, *halves, total)

    shares = lax.all_to_all(total, "mpo", split_axis=0, concat_axis=0, tiled=True)
    return shares.sum(0)


def solution(mesh):
    in_specs = (
        P("sec", None, None),
        P("sec", None),
        P("mpo", "sec", None, None),
        P("mpo", "sec", None, None),
        P("mpo", "sec"),
        P("mpo", "sec"),
    )
    out_specs = P("sec", "mpo", None)
    return jax.shard_map(
        on_device, mesh=mesh, in_specs=in_specs, out_specs=out_specs, check_vma=False
    )
```

time: 93.1 us -> 56.7 us (0.61); the launches traced: 91.3 us -> 56.4 us
  waiting for transfers between devices: 44.6 us -> 5.07 us
  blocking collectives: 0 us -> 19.8 us
  between operations: 13.5 us -> 0.04 us
  Pallas kernels: 0 us -> 8.36 us
  matrix products: 5.81 us -> 0 us
  other arithmetic: 3.41 us -> 0.66 us
  local copies, waits for them, and re-layouts: 4.6 us -> 3.08 us
    reduce_scatter x1 -> x0, waiting for transfers between devices: 40.4 us -> none  [on_device(): lax.psum_scatter(partial_value, 'mpo', scatter_dimension=1, tiled=True)]
    all_to_all x0 -> x1, blocking collectives: none -> 19.8 us  [on_device(): lax.all_to_all(total, 'mpo', split_axis=0, concat_axis=0, tiled=True)]
    pallas_call x0 -> x3, Pallas kernels: none -> 8.36 us  [the longest x1 4.59 us: on_device(): pl.pallas_call(near_kernel, out_shape=[f32] + [bf16] * 4, in_specs=[smem]...]
    dot_general x2 -> x0, matrix products: 5.81 us -> none  [the longest x1 3.39 us: on_device(): jnp.einsum('wkab,wkbc->wkac', left_env, chosen, precision=lax.Precision.H...]
    select_n x2 -> x0, other arithmetic: 1.87 us -> none  [the longest x1 1.18 us: on_device(): masked = jnp.where(keep_mask, wavefunction, jnp.zeros_like(wavefunction))]
    gather x1 -> x0, local copies, waits for them, and re-layouts: 1.82 us -> none  [on_device(): chosen = gathered[position] * mpo_coeffs[:, :, None, None]]
    unnamed x9 -> x8, local copies, waits for them, and re-layouts: 1.58 us -> 3.08 us
    concatenate x1 -> x0, other arithmetic: 1.46 us -> none  [with_halo(): value = jnp.concatenate([before, value, after], axis=dim)]
  transfers between devices with their start and end apart: 3 -> 2, of which waited for: 3 -> 1; matrix products, arithmetic and copies ran while one was open for 2% -> 0% of each run, Pallas kernels for 0% -> 8%
where the time goes in v1:
time: 56.7 us; the launch traced here: 56.4 us
  blocking collectives  19.8 us (35%)
  starting transfers between devices  19.3 us (34%)
  Pallas kernels  8.36 us (15%)
  waiting for transfers between devices  5.07 us (9%)
  local copies, waits for them, and re-layouts  3.08 us (5%)
  other arithmetic  0.66 us (1%)
    all_to_all x1, blocking collectives, on_device(): lax.all_to_all(total, 'mpo', split_axis=0, concat_axis=0, tiled=True)  19.8 us
    ppermute x1, starting transfers between devices, on_device(): lax.ppermute(masked, 'sec', [(i + 1, i) for i in range(devices - 1)])  17.4 us
    ppermute x1, waiting for transfers between devices, on_device(): lax.ppermute(masked, 'sec', [(i + 1, i) for i in range(devices - 1)])  5.07 us
    pallas_call x1, Pallas kernels, on_device(): pl.pallas_call(near_kernel, out_shape=[f32] + [bf16] * 4, in_specs=[smem]...  4.59 us
    unnamed x8, local copies, waits for them, and re-layouts  3.08 us
    ppermute x1, starting transfers between devices, on_device(): lax.ppermute(masked, 'sec', [(i, i + 1) for i in range(devices - 1)])  1.92 us
    pallas_call x1, Pallas kernels, on_device(): pl.pallas_call(mask_kernel, out_shape=jax.ShapeDtypeStruct(wavefunction.s...  1.9 us
    pallas_call x1, Pallas kernels, on_device(): pl.pallas_call(far_kernel, out_shape=f32, in_specs=[smem] * 3 + [vmem] *...  1.87 us
  transfers between devices with their start and end apart: 2, of which 1 were waited for; matrix products, arithmetic and copies ran while one was open for 0% of the time, Pallas kernels for 8%

profile of v1, /device:TPU:112, one launch (start us, length us, event | category | flops | bytes accessed | tf_op | source)
XLA Modules:
  0.0 56.4 jit_solution(929747275824229536)
XLA Ops:
  0.0 1.9 %mask.1.own_ref = f32[2,256,256]{2,1,0:T(8,128)} custom-call(s32[2,2]{1,0:T(2,128)} %sizes_ref.5, f32[2,256,256]{2,1,0:T(8,128)} %wave_ref.1), custom_call_target="tpu_custom_call" | custom-call | tf_op jit(solution)/shard_map/mask/pallas_call | solution.py:104
  1.9 17.4 %collective-permute-start.1 = (f32[2,256,256]{2,1,0:T(8,128)}, f32[2,256,256]{2,1,0:T(8,128)S(1)}, u32[]{:S(2)}, u32[]{:S(2)}) collective-permute-start(f32[2,256,256]{2,1,0:T(8,128)} %mask.1.own_ref), channel_id=1, source_target_pairs={{8,0},{16,8},{24,16},{32,24},{40,32},{48,40},{56,48},{64,56},{72,6... | collective-permute-start | bytes 1572872 | tf_op jit(solution)/shard_map/ppermute | solution.py:112
  19.3 1.9 %collective-permute-start = (f32[2,256,256]{2,1,0:T(8,128)}, f32[2,256,256]{2,1,0:T(8,128)S(1)}, u32[]{:S(2)}, u32[]{:S(2)}) collective-permute-start(f32[2,256,256]{2,1,0:T(8,128)} %mask.1.own_ref), channel_id=1, source_target_pairs={{0,8},{8,16},{16,24},{24,32},{32,40},{40,48},{48,56},{56,64},{64,7... | collective-permute-start | bytes 1572872 | tf_op jit(solution)/shard_map/ppermute | solution.py:113
  21.2 5.1 %collective-permute-done.1.after_ref = f32[2,256,256]{2,1,0:T(8,128)S(1)} collective-permute-done((f32[2,256,256]{2,1,0:T(8,128)}, f32[2,256,256]{2,1,0:T(8,128)S(1)}, u32[]{:S(2)}, u32[]{:S(2)}) %collective-permute-start.1) | collective-permute-done | bytes 524320 | tf_op jit(solution)/shard_map/ppermute | solution.py:112
  26.3 0.0 copy-start
  26.3 1.0 %copy-done = f32[2,256,256]{2,1,0:T(8,128)S(1)} copy-done((f32[2,256,256]{2,1,0:T(8,128)S(1)}, f32[2,256,256]{2,1,0:T(8,128)}, u32[]{:S(2)}) %copy-start) | copy-done | bytes 524312
  27.4 0.0 copy-start.1
  27.4 0.7 %copy-done.1 = s32[2,2]{1,0:T(2,128)S(1)} copy-done((s32[2,2]{1,0:T(2,128)S(1)}, s32[2,2]{1,0:T(2,128)}, u32[]{:S(2)}) %copy-start.1) | copy-done | bytes 40
  28.0 0.0 copy-start.2
  28.0 0.7 %copy-done.2 = f32[3,2]{0,1:T(2,128)S(1)} copy-done((f32[3,2]{0,1:T(2,128)S(1)}, f32[3,2]{0,1:T(2,128)}, u32[]{:S(2)}) %copy-start.2) | copy-done | bytes 48
  28.7 0.0 copy-start.3
  28.7 0.7 %copy-done.3 = s32[3,2]{0,1:T(2,128)S(1)} copy-done((s32[3,2]{0,1:T(2,128)S(1)}, s32[3,2]{0,1:T(2,128)}, u32[]{:S(2)}) %copy-start.3) | copy-done | bytes 48
  29.4 4.6 %near_terms.1 = (f32[8,2,32,256]{3,2,1,0:T(8,128)S(1)}, bf16[3,2,256,256]{3,2,1,0:T(8,128)(2,1)S(1)}, bf16[3,2,256,256]{3,2,1,0:T(8,128)(2,1)S(1)}, bf16[3,2,256...) custom-call(s32[2,2]{1,0:T(2,128)S(1)} %copy-done.1, f32[2,3]{1,0:T(2,128)S(1)} %bitcast.2, s32[2,3]{1,0:T(2,128)S(1)} %bitcast.4, ...), custom_call_target="tpu_custom_call" | custom-call | flops 1207959552 | bytes 8388608 | tf_op jit(solution)/shard_map/near_terms/pallas_call | solution.py:115
  34.0 0.0 collective-permute-done.before_ref
  34.0 1.9 %far_terms.1 = f32[8,2,32,256]{3,2,1,0:T(8,128)S(1)} custom-call(s32[2,2]{1,0:T(2,128)S(1)} %copy-done.1, f32[2,3]{1,0:T(2,128)S(1)} %bitcast.3, s32[2,3]{1,0:T(2,128)S(1)} %bitcast.5, f32[2,256,256]{2,1,0:T(8,128)S(1)} %collective-permute-done.before_ref, bf16[3,2,256,256]{3,2,1,0:T(8,128)(2,1)S(1)} %get-tuple-element.10.left_high, ...), custom_call_target="tpu_custom_call" | custom-call | flops 402653184 | bytes 4194304 | tf_op jit(solution)/shard_map/far_terms/pallas_call | solution.py:127
  35.9 19.8 %all_to_all.5 = f32[8,2,32,256]{3,2,1,0:T(8,128)S(1)} all-to-all(f32[8,2,32,256]{3,2,1,0:T(8,128)S(1)} %far_terms.1), channel_id=1, replica_groups=mesh['sec'=128,'mpo'=8] {'mpo'}, dimensions={0} | all-to-all | bytes 1048576 | tf_op jit(solution)/shard_map/all_to_all | solution.py:139
  55.7 0.7 %reduce_sum.9 = f32[2,32,256]{2,1,0:T(8,128)} reduce(f32[8,2,32,256]{3,2,1,0:T(8,128)S(1)} %all_to_all.5, f32[]{:T(128)} %constant.0.clone.1), dimensions={0}, to_apply=%region_0.0 | reduce | flops 114688 | bytes 589828 | tf_op jit(solution)/shard_map/reduce_sum | solution.py:140
Async XLA Ops:
  1.9 24.4 %collective-permute-start.1 = (f32[2,256,256]{2,1,0:T(8,128)}, f32[2,256,256]{2,1,0:T(8,128)S(1)}, u32[]{:S(2)}, u32[]{:S(2)}) collective-permute-start(f32[2,256,256]{2,1,0:T(8,128)} %mask.1.own_ref), channel_id=1, source_target_pairs={{8,0},{16,8},{24,16},{32,24},{40,32},{48,40},{56,48},{64,56},{72,6... | collective-permute-start | bytes 1572872 | tf_op jit(solution)/shard_map/ppermute | solution.py:112
  19.3 14.7 %collective-permute-start = (f32[2,256,256]{2,1,0:T(8,128)}, f32[2,256,256]{2,1,0:T(8,128)S(1)}, u32[]{:S(2)}, u32[]{:S(2)}) collective-permute-start(f32[2,256,256]{2,1,0:T(8,128)} %mask.1.own_ref), channel_id=1, source_target_pairs={{0,8},{8,16},{16,24},{24,32},{32,40},{40,48},{48,56},{56,64},{64,7... | collective-permute-start | bytes 1572872 | tf_op jit(solution)/shard_map/ppermute | solution.py:113
  26.3 1.0 %copy-start = (f32[2,256,256]{2,1,0:T(8,128)S(1)}, f32[2,256,256]{2,1,0:T(8,128)}, u32[]{:S(2)}) copy-start(f32[2,256,256]{2,1,0:T(8,128)} %mask.1.own_ref) | copy-start | bytes 1572868
  27.4 0.7 %copy-start.1 = (s32[2,2]{1,0:T(2,128)S(1)}, s32[2,2]{1,0:T(2,128)}, u32[]{:S(2)}) copy-start(s32[2,2]{1,0:T(2,128)} %sizes_ref.5) | copy-start | bytes 52
  28.0 0.7 %copy-start.2 = (f32[3,2]{0,1:T(2,128)S(1)}, f32[3,2]{0,1:T(2,128)}, u32[]{:S(2)}) copy-start(f32[3,2]{0,1:T(2,128)} %param.10) | copy-start | bytes 76
  28.7 0.7 %copy-start.3 = (s32[3,2]{0,1:T(2,128)S(1)}, s32[3,2]{0,1:T(2,128)}, u32[]{:S(2)}) copy-start(s32[3,2]{0,1:T(2,128)} %param.11) | copy-start | bytes 76

commit v2 on v1

v2 whole, which is shorter than its diff:
```python
import functools

import jax
import jax.numpy as jnp
from jax import lax
from jax.experimental import pallas as pl
from jax.experimental.pallas import tpu as pltpu
from jax.sharding import PartitionSpec as P

VMEM_LIMIT = 40 * 1024 * 1024
vmem = pl.BlockSpec(memory_space=pltpu.VMEM)
smem = pl.BlockSpec(memory_space=pltpu.SMEM)
hbm = pl.BlockSpec(memory_space=pltpu.HBM)


def inside(limit, shape, dim):
    return lax.broadcasted_iota(jnp.int32, shape, dim) < limit


def split(value):
    high = value.astype(jnp.bfloat16)
    return high, (value - high.astype(jnp.float32)).astype(jnp.bfloat16)


def product(left, right, contract):
    (left_high, left_low), (right_high, right_low) = left, right
    return lax.dot_general(
        jnp.concatenate([left_high, left_low, left_high], axis=1),
        jnp.concatenate([right_high, right_high, right_low], axis=contract),
        dimension_numbers=(((1,), (contract,)), ((), ())),
        preferred_element_type=jnp.float32,
    )


def mask_kernel(sizes_hbm, wave_hbm, masked_ref, sizes_ref, wave_ref, small, large):
    blocks, rows, columns = wave_ref.shape
    shape = (rows, columns)
    sizes = pltpu.make_async_copy(sizes_hbm, sizes_ref, small)
    sizes.start()
    loads = [
        pltpu.make_async_copy(wave_hbm.at[k], wave_ref.at[k], large.at[k]) for k in range(blocks)
    ]
    for load in loads:
        load.start()
    sizes.wait()
    for k, load in enumerate(loads):
        load.wait()
        keep = inside(sizes_ref[k, 0], shape, 0) & inside(sizes_ref[k, 1], shape, 1)
        masked_ref[k] = jnp.where(keep, wave_ref[k], 0.0)


def own_kernel(
    sizes_hbm, coeff_hbm, source_hbm, masked_ref, left_hbm, right_hbm,
    total_ref, left_high, left_low, right_high, right_low, list_ref,
    sizes_ref, coeff_ref, source_ref, left_ref, right_ref, small, large,
):
    pairs = [(sizes_hbm, sizes_ref), (coeff_hbm, coeff_ref), (source_hbm, source_ref)]
    copies = [pltpu.make_async_copy(*pair, small.at[i]) for i, pair in enumerate(pairs)]
    for copy in copies:
        copy.start()
    terms, blocks, rows, columns = left_ref.shape
    loads = {}
    for k in range(blocks):
        for w in range(terms):
            at = (w, k)
            loads[at] = (
                pltpu.make_async_copy(left_hbm.at[at], left_ref.at[at], large.at[0, w, k]),
                pltpu.make_async_copy(right_hbm.at[at], right_ref.at[at], large.at[1, w, k]),
            )
            for load in loads[at]:
                load.start()
    parts, _, part, _ = total_ref.shape
    shape = (rows, columns)
    total_ref[...] = jnp.zeros_like(total_ref)
    for copy in copies:
        copy.wait()
    first = lax.axis_index("sec") * blocks
    for k in range(blocks):
        count = jnp.int32(0)
        for w in range(terms):
            place = source_ref[k, w] - first
            mine = (place >= 0) & (place < blocks)
            for load in loads[w, k]:
                load.wait()
            scaled = left_ref[w, k] * coeff_ref[k, w]
            left = split(jnp.where(inside(sizes_ref[k, 0], shape, 0), scaled, 0.0))
            right = split(jnp.where(inside(sizes_ref[k, 1], shape, 0), right_ref[w, k], 0.0))

            @pl.when(mine)
            def _():
                chosen = masked_ref[jnp.clip(place, 0, blocks - 1)]
                done = product(left, split(chosen), 0)
                term = product(split(done), right, 1)
                total_ref[:, k] += term.reshape(parts, part, columns)

            @pl.when(~mine)
            def _(count=count):
                list_ref[k, count] = w
                list_ref[k, terms + count] = jnp.where(place < 0, place + blocks, place)
                left_high[w, k], left_low[w, k] = left
                right_high[w, k], right_low[w, k] = right

            count = count + jnp.where(mine, 0, 1)
        list_ref[k, 2 * terms] = count


def other_kernel(
    list_ref, after_ref, before_ref, left_high, left_low, right_high, right_low, sum_ref,
    total_ref, high_ref, low_ref,
):
    terms, blocks, rows, columns = left_high.shape
    parts, _, part, _ = total_ref.shape
    for i in range(2 * blocks):
        value = before_ref[i] if i < blocks else after_ref[i - blocks]
        high_ref[i], low_ref[i] = split(value)
    total_ref[...] = sum_ref[...]
    counts = [list_ref[k, 2 * terms] for k in range(blocks)]
    both = functools.reduce(jnp.minimum, counts)

    def term(k, j):
        w = jnp.clip(list_ref[k, j], 0, terms - 1)
        i = jnp.clip(list_ref[k, terms + j], 0, 2 * blocks - 1)
        done = product((left_high[w, k], left_low[w, k]), (high_ref[i], low_ref[i]), 0)
        return product(split(done), (right_high[w, k], right_low[w, k]), 1)

    for j in range(terms):

        @pl.when(j < both)
        def _():
            results = [term(k, j) for k in range(blocks)]
            for k in range(blocks):
                total_ref[:, k] += results[k].reshape(parts, part, columns)

        for k in range(blocks):

            @pl.when((j >= both) & (j < counts[k]))
            def _():
                total_ref[:, k] += term(k, j).reshape(parts, part, columns)


def on_device(wavefunction, sector_sizes, left_env, right_env, mpo_coeffs, source_block):
    blocks, rows, columns = wavefunction.shape
    terms = left_env.shape[0]
    devices, parts = lax.axis_size("sec"), lax.axis_size("mpo")
    coeffs, sources = mpo_coeffs.T, source_block.T
    params = pltpu.CompilerParams(vmem_limit_bytes=VMEM_LIMIT)
    share = jax.ShapeDtypeStruct((parts, blocks, rows // parts, columns), jnp.float32)
    half = jax.ShapeDtypeStruct((terms, blocks, rows, columns), jnp.bfloat16)
    up = [(i, i + 1) for i in range(devices - 1)]
    down = [(j, i) for i, j in up]

    cost = pl.CostEstimate(flops=10**10, bytes_accessed=1, transcendentals=0)

    masked = pl.pallas_call(
        mask_kernel,
        out_shape=pltpu.VMEM(wavefunction.shape, jnp.float32),
        in_specs=[hbm, hbm],
        out_specs=vmem,
        scratch_shapes=[
            pltpu.SMEM(sector_sizes.shape, jnp.int32),
            pltpu.VMEM(wavefunction.shape, jnp.float32),
            pltpu.SemaphoreType.DMA,
            pltpu.SemaphoreType.DMA((blocks,)),
        ],
        cost_estimate=cost,
        name="mask",
    )(sector_sizes, wavefunction)

    before = lax.ppermute(masked, "sec", up)
    after = lax.ppermute(masked, "sec", down)

    total, *halves, others = pl.pallas_call(
        own_kernel,
        out_shape=[share] + [half] * 4 + [jax.ShapeDtypeStruct((blocks, 8), jnp.int32)],
        in_specs=[hbm] * 3 + [vmem] + [hbm] * 2,
        out_specs=[vmem] * 5 + [smem],
        scratch_shapes=[
            pltpu.SMEM(sector_sizes.shape, jnp.int32),
            pltpu.SMEM(coeffs.shape, jnp.float32),
            pltpu.SMEM(sources.shape, jnp.int32),
            pltpu.VMEM(left_env.shape, jnp.float32),
            pltpu.VMEM(right_env.shape, jnp.float32),
            pltpu.SemaphoreType.DMA((3,)),
            pltpu.SemaphoreType.DMA((2, terms, blocks)),
        ],
        compiler_params=params,
        cost_estimate=cost,
        name="own_terms",
    )(sector_sizes, coeffs, sources, masked, left_env, right_env)

    total = pl.pallas_call(
        other_kernel,
        out_shape=share,
        in_specs=[smem] + [vmem] * 7,
        out_specs=vmem,
        scratch_shapes=[pltpu.VMEM((2 * blocks, rows, columns), jnp.bfloat16)] * 2,
        compiler_params=params,
        cost_estimate=cost,
        name="other_terms",
    )(others, after, before, *halves, total)

    shares = lax.all_to_all(total, "mpo", split_axis=0, concat_axis=0, tiled=True)
    return shares.sum(0)


def solution(mesh):
    in_specs = (
        P("sec", None, None),
        P("sec", None),
        P("mpo", "sec", None, None),
        P("mpo", "sec", None, None),
        P("mpo", "sec"),
        P("mpo", "sec"),
    )
    out_specs = P("sec", "mpo", None)
    return jax.shard_map(
        on_device, mesh=mesh, in_specs=in_specs, out_specs=out_specs, check_vma=False
    )
```

time: 56.7 us -> 50.4 us (0.89)
  waiting for transfers between devices: 5.07 us -> 1.66 us
  local copies, waits for them, and re-layouts: 3.08 us -> 1.42 us
  Pallas kernels: 8.36 us -> 7.14 us
    ppermute x2, waiting for transfers between devices: 5.07 us -> 1.66 us  [the longest x1 1.65 us: on_device(): after = lax.ppermute(masked, 'sec', down)]
    unnamed x8 -> x10, local copies, waits for them, and re-layouts: 3.08 us -> 1.42 us
    pallas_call x3, Pallas kernels: 8.36 us -> 7.14 us  [the longest x1 3.55 us: on_device(): pl.pallas_call(own_kernel, out_shape=[share] + [half] * 4 + [jax.ShapeDty...]
  transfers between devices with their start and end apart: 2 -> 2, of which waited for: 1 -> 1; matrix products, arithmetic and copies ran while one was open for 0% -> 0% of each run, Pallas kernels for 8% -> 7%
where the time goes in v2:
time: 50.4 us; the launch traced here: 50.2 us
  blocking collectives  19.8 us (39%)
  starting transfers between devices  19.3 us (38%)
  Pallas kernels  7.14 us (14%)
  waiting for transfers between devices  1.66 us (3%)
  local copies, waits for them, and re-layouts  1.42 us (3%)
  other arithmetic  0.66 us (1%)
    all_to_all x1, blocking collectives, on_device(): lax.all_to_all(total, 'mpo', split_axis=0, concat_axis=0, tiled=True)  19.8 us
    ppermute x1, starting transfers between devices, on_device(): after = lax.ppermute(masked, 'sec', down)  17.4 us
    pallas_call x1, Pallas kernels, on_device(): pl.pallas_call(own_kernel, out_shape=[share] + [half] * 4 + [jax.ShapeDty...  3.55 us
    pallas_call x1, Pallas kernels, on_device(): pl.pallas_call(other_kernel, out_shape=share, in_specs=[smem] + [vmem] *...  2.39 us
    ppermute x1, starting transfers between devices, on_device(): before = lax.ppermute(masked, 'sec', up)  1.92 us
    ppermute x1, waiting for transfers between devices, on_device(): after = lax.ppermute(masked, 'sec', down)  1.65 us
    unnamed x10, local copies, waits for them, and re-layouts  1.42 us
    pallas_call x1, Pallas kernels, on_device(): pl.pallas_call(mask_kernel, out_shape=pltpu.VMEM(wavefunction.shape, jnp....  1.2 us
  transfers between devices with their start and end apart: 2, of which 1 were waited for; matrix products, arithmetic and copies ran while one was open for 0% of the time, Pallas kernels for 7%

profile of v2, /device:TPU:112, one launch (start us, length us, event | category | flops | bytes accessed | tf_op | source)
XLA Modules:
  0.0 50.2 jit_solution(2126952174736266314)
XLA Ops:
  0.0 0.0 copy-start.2
  0.0 0.0 copy-start.4
  0.0 0.0 copy-start.3
  0.0 0.0 copy-start
  0.0 1.2 %mask.1.masked_ref = f32[2,256,256]{2,1,0:T(8,128)S(1)} custom-call(s32[2,2]{1,0:T(2,128)} %sizes_hbm.3, f32[2,256,256]{2,1,0:T(8,128)} %wave_hbm.1), custom_call_target="tpu_custom_call" | custom-call | flops 10000000000 | bytes 1 | tf_op jit(solution)/shard_map/mask/pallas_call | solution.py:154
  1.2 1.9 %collective-permute-start.1 = (f32[2,256,256]{2,1,0:T(8,128)S(1)}, f32[2,256,256]{2,1,0:T(8,128)S(1)}, u32[]{:S(2)}, u32[]{:S(2)}) collective-permute-start(f32[2,256,256]{2,1,0:T(8,128)S(1)} %mask.1.masked_ref), channel_id=1, source_target_pairs={{0,8},{8,16},{16,24},{24,32},{32,40},{40,48},{48,56},{56,64},{64,7... | collective-permute-start | bytes 1572872 | tf_op jit(solution)/shard_map/ppermute | solution.py:169
  3.2 17.4 %collective-permute-start = (f32[2,256,256]{2,1,0:T(8,128)S(1)}, f32[2,256,256]{2,1,0:T(8,128)S(1)}, u32[]{:S(2)}, u32[]{:S(2)}) collective-permute-start(f32[2,256,256]{2,1,0:T(8,128)S(1)} %mask.1.masked_ref), channel_id=1, source_target_pairs={{8,0},{16,8},{24,16},{32,24},{40,32},{48,40},{56,48},{64,56},{72,6... | collective-permute-start | bytes 1572872 | tf_op jit(solution)/shard_map/ppermute | solution.py:170
  20.6 0.0 copy-done.2
  20.6 0.0 copy-done.4
  20.6 0.0 copy-done.3
  20.6 0.0 copy-done
  20.6 0.0 copy-start.1
  20.6 1.4 %copy-done.1 = f32[3,2,256,256]{3,2,1,0:T(8,128)S(1)} copy-done((f32[3,2,256,256]{3,2,1,0:T(8,128)S(1)}, f32[3,2,256,256]{3,2,1,0:T(8,128)}, u32[]{:S(2)}) %copy-start.1) | copy-done | bytes 1572888
  22.0 3.6 %own_terms.1 = (f32[8,2,32,256]{3,2,1,0:T(8,128)S(1)}, bf16[3,2,256,256]{3,2,1,0:T(8,128)(2,1)S(1)}, bf16[3,2,256,256]{3,2,1,0:T(8,128)(2,1)S(1)}, bf16[3,2,256,...) custom-call(s32[2,2]{1,0:T(2,128)S(1)} %copy-done.2, f32[2,3]{1,0:T(2,128)S(1)} %bitcast.2, ...), custom_call_target="tpu_custom_call" | custom-call | flops 10000000000 | bytes 1 | tf_op jit(solution)/shard_map/own_terms/pallas_call | solution.py:172
  25.6 0.0 collective-permute-done.1.before_ref
  25.6 1.7 %collective-permute-done.after_ref = f32[2,256,256]{2,1,0:T(8,128)S(1)} collective-permute-done((f32[2,256,256]{2,1,0:T(8,128)S(1)}, f32[2,256,256]{2,1,0:T(8,128)S(1)}, u32[]{:S(2)}, u32[]{:S(2)}) %collective-permute-start) | collective-permute-done | bytes 524320 | tf_op jit(solution)/shard_map/ppermute | solution.py:170
  27.3 2.4 %other_terms.1 = f32[8,2,32,256]{3,2,1,0:T(8,128)S(1)} custom-call(s32[2,8]{1,0:T(2,128)S(1)} %get-tuple-element.11.list_ref, f32[2,256,256]{2,1,0:T(8,128)S(1)} %collective-permute-done.after_ref, f32[2,256,256]{2,1,0:T(8,128)S(1)} %collective-permute-done.1.before_ref, bf16[3,2,256,256]{3,2,1,0:T(8,128)(2,1)S(1)} %get-tuple-element.12.left_high, ...), custom_call_target="tpu_custom_call" | custom-call | flops 10000000000 | bytes 1 | tf_op jit(solution)/shard_map/other_terms/pallas_call | solution.py:191
  29.7 19.8 %all_to_all.5 = f32[8,2,32,256]{3,2,1,0:T(8,128)S(1)} all-to-all(f32[8,2,32,256]{3,2,1,0:T(8,128)S(1)} %other_terms.1), channel_id=1, replica_groups=mesh['sec'=128,'mpo'=8] {'mpo'}, dimensions={0} | all-to-all | bytes 1048576 | tf_op jit(solution)/shard_map/all_to_all | solution.py:202
  49.5 0.7 %reduce_sum.9 = f32[2,32,256]{2,1,0:T(8,128)} reduce(f32[8,2,32,256]{3,2,1,0:T(8,128)S(1)} %all_to_all.5, f32[]{:T(128)} %constant.0.clone.1), dimensions={0}, to_apply=%region_0.0 | reduce | flops 114688 | bytes 589828 | tf_op jit(solution)/shard_map/reduce_sum | solution.py:203
Async XLA Ops:
  0.0 20.6 %copy-start.2 = (s32[2,2]{1,0:T(2,128)S(1)}, s32[2,2]{1,0:T(2,128)}, u32[]{:S(2)}) copy-start(s32[2,2]{1,0:T(2,128)} %sizes_hbm.3) | copy-start | bytes 52
  0.0 20.6 %copy-start.4 = (s32[3,2]{0,1:T(2,128)S(1)}, s32[3,2]{0,1:T(2,128)}, u32[]{:S(2)}) copy-start(s32[3,2]{0,1:T(2,128)} %param.11) | copy-start | bytes 76
  0.0 20.6 %copy-start.3 = (f32[3,2]{0,1:T(2,128)S(1)}, f32[3,2]{0,1:T(2,128)}, u32[]{:S(2)}) copy-start(f32[3,2]{0,1:T(2,128)} %param.10) | copy-start | bytes 76
  0.0 20.6 %copy-start = (f32[3,2,256,256]{3,2,1,0:T(8,128)S(1)}, f32[3,2,256,256]{3,2,1,0:T(8,128)}, u32[]{:S(2)}) copy-start(f32[3,2,256,256]{3,2,1,0:T(8,128)} %left_hbm.1) | copy-start | bytes 4718596
  1.2 24.4 %collective-permute-start.1 = (f32[2,256,256]{2,1,0:T(8,128)S(1)}, f32[2,256,256]{2,1,0:T(8,128)S(1)}, u32[]{:S(2)}, u32[]{:S(2)}) collective-permute-start(f32[2,256,256]{2,1,0:T(8,128)S(1)} %mask.1.masked_ref), channel_id=1, source_target_pairs={{0,8},{8,16},{16,24},{24,32},{32,40},{40,48},{48,56},{56,64},{64,7... | collective-permute-start | bytes 1572872 | tf_op jit(solution)/shard_map/ppermute | solution.py:169
  3.2 24.1 %collective-permute-start = (f32[2,256,256]{2,1,0:T(8,128)S(1)}, f32[2,256,256]{2,1,0:T(8,128)S(1)}, u32[]{:S(2)}, u32[]{:S(2)}) collective-permute-start(f32[2,256,256]{2,1,0:T(8,128)S(1)} %mask.1.masked_ref), channel_id=1, source_target_pairs={{8,0},{16,8},{24,16},{32,24},{40,32},{48,40},{56,48},{64,56},{72,6... | collective-permute-start | bytes 1572872 | tf_op jit(solution)/shard_map/ppermute | solution.py:170
  20.6 1.4 %copy-start.1 = (f32[3,2,256,256]{3,2,1,0:T(8,128)S(1)}, f32[3,2,256,256]{3,2,1,0:T(8,128)}, u32[]{:S(2)}) copy-start(f32[3,2,256,256]{3,2,1,0:T(8,128)} %right_hbm.1) | copy-start | bytes 4718596

commit v3 on v2

--- a/solution.py
+++ b/solution.py
@@ -20,6 +20,15 @@
 def split(value):
     high = value.astype(jnp.bfloat16)
     return high, (value - high.astype(jnp.float32)).astype(jnp.bfloat16)
+
+
+def order(parts):
+    return [(parts // 2 - x) % parts for x in range(parts)]
+
+
+def arranged(value, parts):
+    part = value.shape[0] // parts
+    return jnp.stack([value[x * part : (x + 1) * part] for x in order(parts)])
 
 
 def product(left, right, contract):
@@ -91,7 +100,7 @@
                 chosen = masked_ref[jnp.clip(place, 0, blocks - 1)]
                 done = product(left, split(chosen), 0)
                 term = product(split(done), right, 1)
-                total_ref[:, k] += term.reshape(parts, part, columns)
+                total_ref[:, k] += arranged(term, parts)
 
             @pl.when(~mine)
             def _(count=count):
@@ -113,29 +122,44 @@
     for i in range(2 * blocks):
         value = before_ref[i] if i < blocks else after_ref[i - blocks]
         high_ref[i], low_ref[i] = split(value)
-    total_ref[...] = sum_ref[...]
     counts = [list_ref[k, 2 * terms] for k in range(blocks)]
     both = functools.reduce(jnp.minimum, counts)
 
-    def term(k, j):
+    def first_product(k, j):
         w = jnp.clip(list_ref[k, j], 0, terms - 1)
         i = jnp.clip(list_ref[k, terms + j], 0, 2 * blocks - 1)
         done = product((left_high[w, k], left_low[w, k]), (high_ref[i], low_ref[i]), 0)
-        return product(split(done), (right_high[w, k], right_low[w, k]), 1)
-
-    for j in range(terms):
-
-        @pl.when(j < both)
-        def _():
-            results = [term(k, j) for k in range(blocks)]
-            for k in range(blocks):
-                total_ref[:, k] += results[k].reshape(parts, part, columns)
-
+        return split(done), (right_high[w, k], right_low[w, k])
+
+    def sum_of_terms(k, places):
+        pairs = [first_product(k, j) for j in places]
+        left, right = (
+            tuple(jnp.concatenate([pair[side][part] for pair in pairs], axis=1) for part in (0, 1))
+            for side in (0, 1)
+        )
+        return arranged(product(left, right, 1), parts)
+
+    @pl.when(both >= 2)
+    def _():
         for k in range(blocks):
-
-            @pl.when((j >= both) & (j < counts[k]))
+            total_ref[:, k] = sum_ref[:, k] + sum_of_terms(k, (0, 1))
+
+    @pl.when(both < 2)
+    def _():
+        total_ref[...] = sum_ref[...]
+        for k in range(blocks):
+            for j in range(min(2, terms)):
+
+                @pl.when(j < counts[k])
+                def _():
+                    total_ref[:, k] += sum_of_terms(k, (j,))
+
+    for j in range(2, terms):
+        for k in range(blocks):
+
+            @pl.when(j < counts[k])
             def _():
-                total_ref[:, k] += term(k, j).reshape(parts, part, columns)
+                total_ref[:, k] += sum_of_terms(k, (j,))
 
 
 def on_device(wavefunction, sector_sizes, left_env, right_env, mpo_coeffs, source_block):
@@ -199,7 +223,7 @@
         name="other_terms",
     )(others, after, before, *halves, total)
 
-    shares = lax.all_to_all(total, "mpo", split_axis=0, concat_axis=0, tiled=True)
+    shares = lax.all_to_all(total, "mpo", split_axis=0, concat_axis=0, tiled=True, axis_index_groups=[order(parts)])
     return shares.sum(0)
 
 

time: 50.4 us -> 46 us (0.913)
  blocking collectives: 19.8 us -> 15.5 us
    all_to_all x1, blocking collectives: 19.8 us -> 15.5 us  [on_device(): lax.all_to_all(total, 'mpo', split_axis=0, concat_axis=0, tiled=True, axi...]
  transfers between devices with their start and end apart: 2 -> 2, of which waited for: 1 -> 1; matrix products, arithmetic and copies ran while one was open for 0% -> 0% of each run, Pallas kernels for 7% -> 8%
where the time goes in v3:
time: 46 us; the launch traced here: 45.5 us
  starting transfers between devices  19.3 us (42%)
  blocking collectives  15.5 us (34%)
  Pallas kernels  6.86 us (15%)
  waiting for transfers between devices  1.66 us (4%)
  local copies, waits for them, and re-layouts  1.42 us (3%)
  other arithmetic  0.66 us (1%)
    ppermute x1, starting transfers between devices, on_device(): after = lax.ppermute(masked, 'sec', down)  17.4 us
    all_to_all x1, blocking collectives, on_device(): lax.all_to_all(total, 'mpo', split_axis=0, concat_axis=0, tiled=True, axi...  15.5 us
    pallas_call x1, Pallas kernels, on_device(): pl.pallas_call(own_kernel, out_shape=[share] + [half] * 4 + [jax.ShapeDty...  3.55 us
    pallas_call x1, Pallas kernels, on_device(): pl.pallas_call(other_kernel, out_shape=share, in_specs=[smem] + [vmem] *...  2.11 us
    ppermute x1, starting transfers between devices, on_device(): before = lax.ppermute(masked, 'sec', up)  1.92 us
    ppermute x1, waiting for transfers between devices, on_device(): after = lax.ppermute(masked, 'sec', down)  1.65 us
    unnamed x10, local copies, waits for them, and re-layouts  1.42 us
    pallas_call x1, Pallas kernels, on_device(): pl.pallas_call(mask_kernel, out_shape=pltpu.VMEM(wavefunction.shape, jnp....  1.2 us
  transfers between devices with their start and end apart: 2, of which 1 were waited for; matrix products, arithmetic and copies ran while one was open for 0% of the time, Pallas kernels for 8%

profile of v3, /device:TPU:112, one launch (start us, length us, event | category | flops | bytes accessed | tf_op | source)
XLA Modules:
  0.0 45.5 jit_solution(17122507952241780282)
XLA Ops:
  0.0 0.0 copy-start.2
  0.0 0.0 copy-start.4
  0.0 0.0 copy-start.3
  0.0 0.0 copy-start
  0.0 1.2 %mask.1.masked_ref = f32[2,256,256]{2,1,0:T(8,128)S(1)} custom-call(s32[2,2]{1,0:T(2,128)} %sizes_hbm.3, f32[2,256,256]{2,1,0:T(8,128)} %wave_hbm.1), custom_call_target="tpu_custom_call" | custom-call | flops 10000000000 | bytes 1 | tf_op jit(solution)/shard_map/mask/pallas_call | solution.py:178
  1.2 1.9 %collective-permute-start.1 = (f32[2,256,256]{2,1,0:T(8,128)S(1)}, f32[2,256,256]{2,1,0:T(8,128)S(1)}, u32[]{:S(2)}, u32[]{:S(2)}) collective-permute-start(f32[2,256,256]{2,1,0:T(8,128)S(1)} %mask.1.masked_ref), channel_id=1, source_target_pairs={{0,8},{8,16},{16,24},{24,32},{32,40},{40,48},{48,56},{56,64},{64,7... | collective-permute-start | bytes 1572872 | tf_op jit(solution)/shard_map/ppermute | solution.py:193
  3.2 17.4 %collective-permute-start = (f32[2,256,256]{2,1,0:T(8,128)S(1)}, f32[2,256,256]{2,1,0:T(8,128)S(1)}, u32[]{:S(2)}, u32[]{:S(2)}) collective-permute-start(f32[2,256,256]{2,1,0:T(8,128)S(1)} %mask.1.masked_ref), channel_id=1, source_target_pairs={{8,0},{16,8},{24,16},{32,24},{40,32},{48,40},{56,48},{64,56},{72,6... | collective-permute-start | bytes 1572872 | tf_op jit(solution)/shard_map/ppermute | solution.py:194
  20.6 0.0 copy-done.2
  20.6 0.0 copy-done.4
  20.6 0.0 copy-done.3
  20.6 0.0 copy-done
  20.6 0.0 copy-start.1
  20.6 1.4 %copy-done.1 = f32[3,2,256,256]{3,2,1,0:T(8,128)S(1)} copy-done((f32[3,2,256,256]{3,2,1,0:T(8,128)S(1)}, f32[3,2,256,256]{3,2,1,0:T(8,128)}, u32[]{:S(2)}) %copy-start.1) | copy-done | bytes 1572888
  22.0 3.6 %own_terms.1 = (f32[8,2,32,256]{3,2,1,0:T(8,128)S(1)}, bf16[3,2,256,256]{3,2,1,0:T(8,128)(2,1)S(1)}, bf16[3,2,256,256]{3,2,1,0:T(8,128)(2,1)S(1)}, bf16[3,2,256,...) custom-call(s32[2,2]{1,0:T(2,128)S(1)} %copy-done.2, f32[2,3]{1,0:T(2,128)S(1)} %bitcast.2, ...), custom_call_target="tpu_custom_call" | custom-call | flops 10000000000 | bytes 1 | tf_op jit(solution)/shard_map/own_terms/pallas_call | solution.py:196
  25.6 0.0 collective-permute-done.1.before_ref
  25.6 1.7 %collective-permute-done.after_ref = f32[2,256,256]{2,1,0:T(8,128)S(1)} collective-permute-done((f32[2,256,256]{2,1,0:T(8,128)S(1)}, f32[2,256,256]{2,1,0:T(8,128)S(1)}, u32[]{:S(2)}, u32[]{:S(2)}) %collective-permute-start) | collective-permute-done | bytes 524320 | tf_op jit(solution)/shard_map/ppermute | solution.py:194
  27.3 2.1 %other_terms.1 = f32[8,2,32,256]{3,2,1,0:T(8,128)S(1)} custom-call(s32[2,8]{1,0:T(2,128)S(1)} %get-tuple-element.11.list_ref, f32[2,256,256]{2,1,0:T(8,128)S(1)} %collective-permute-done.after_ref, f32[2,256,256]{2,1,0:T(8,128)S(1)} %collective-permute-done.1.before_ref, bf16[3,2,256,256]{3,2,1,0:T(8,128)(2,1)S(1)} %get-tuple-element.12.left_high, ...), custom_call_target="tpu_custom_call" | custom-call | flops 10000000000 | bytes 1 | tf_op jit(solution)/shard_map/other_terms/pallas_call | solution.py:215
  29.4 15.5 %all_to_all.5 = f32[8,2,32,256]{3,2,1,0:T(8,128)S(1)} all-to-all(f32[8,2,32,256]{3,2,1,0:T(8,128)S(1)} %other_terms.1), channel_id=1, replica_groups={{4,3,2,1,0,7,6,5},{12,11,10,9,8,15,14,13},{20,19,18,17,16,23,22,21},{28..., dimensions={0} | all-to-all | bytes 1048576 | tf_op jit(solution)/shard_map/all_to_all | solution.py:226
  44.8 0.7 %reduce_sum.9 = f32[2,32,256]{2,1,0:T(8,128)} reduce(f32[8,2,32,256]{3,2,1,0:T(8,128)S(1)} %all_to_all.5, f32[]{:T(128)} %constant.0.clone.1), dimensions={0}, to_apply=%region_0.0 | reduce | flops 114688 | bytes 589828 | tf_op jit(solution)/shard_map/reduce_sum | solution.py:227
Async XLA Ops:
  0.0 20.6 %copy-start.2 = (s32[2,2]{1,0:T(2,128)S(1)}, s32[2,2]{1,0:T(2,128)}, u32[]{:S(2)}) copy-start(s32[2,2]{1,0:T(2,128)} %sizes_hbm.3) | copy-start | bytes 52
  0.0 20.6 %copy-start.4 = (s32[3,2]{0,1:T(2,128)S(1)}, s32[3,2]{0,1:T(2,128)}, u32[]{:S(2)}) copy-start(s32[3,2]{0,1:T(2,128)} %param.11) | copy-start | bytes 76
  0.0 20.6 %copy-start.3 = (f32[3,2]{0,1:T(2,128)S(1)}, f32[3,2]{0,1:T(2,128)}, u32[]{:S(2)}) copy-start(f32[3,2]{0,1:T(2,128)} %param.10) | copy-start | bytes 76
  0.0 20.6 %copy-start = (f32[3,2,256,256]{3,2,1,0:T(8,128)S(1)}, f32[3,2,256,256]{3,2,1,0:T(8,128)}, u32[]{:S(2)}) copy-start(f32[3,2,256,256]{3,2,1,0:T(8,128)} %left_hbm.1) | copy-start | bytes 4718596
  1.2 24.4 %collective-permute-start.1 = (f32[2,256,256]{2,1,0:T(8,128)S(1)}, f32[2,256,256]{2,1,0:T(8,128)S(1)}, u32[]{:S(2)}, u32[]{:S(2)}) collective-permute-start(f32[2,256,256]{2,1,0:T(8,128)S(1)} %mask.1.masked_ref), channel_id=1, source_target_pairs={{0,8},{8,16},{16,24},{24,32},{32,40},{40,48},{48,56},{56,64},{64,7... | collective-permute-start | bytes 1572872 | tf_op jit(solution)/shard_map/ppermute | solution.py:193
  3.2 24.1 %collective-permute-start = (f32[2,256,256]{2,1,0:T(8,128)S(1)}, f32[2,256,256]{2,1,0:T(8,128)S(1)}, u32[]{:S(2)}, u32[]{:S(2)}) collective-permute-start(f32[2,256,256]{2,1,0:T(8,128)S(1)} %mask.1.masked_ref), channel_id=1, source_target_pairs={{8,0},{16,8},{24,16},{32,24},{40,32},{48,40},{56,48},{64,56},{72,6... | collective-permute-start | bytes 1572872 | tf_op jit(solution)/shard_map/ppermute | solution.py:194
  20.6 1.4 %copy-start.1 = (f32[3,2,256,256]{3,2,1,0:T(8,128)S(1)}, f32[3,2,256,256]{3,2,1,0:T(8,128)}, u32[]{:S(2)}) copy-start(f32[3,2,256,256]{3,2,1,0:T(8,128)} %right_hbm.1) | copy-start | bytes 4718596

commit v4 on v3

--- a/solution.py
+++ b/solution.py
@@ -85,7 +85,7 @@
         copy.wait()
     first = lax.axis_index("sec") * blocks
     for k in range(blocks):
-        count = jnp.int32(0)
+        counts = [jnp.int32(0), jnp.int32(0)]
         for w in range(terms):
             place = source_ref[k, w] - first
             mine = (place >= 0) & (place < blocks)
@@ -102,64 +102,62 @@
                 term = product(split(done), right, 1)
                 total_ref[:, k] += arranged(term, parts)
 
+            for side, belongs in enumerate((place < 0, place >= blocks)):
+
+                @pl.when(belongs)
+                def _(side=side, count=counts[side]):
+                    list_ref[k, side * 8 + count] = w
+                    list_ref[k, side * 8 + terms + count] = place + blocks * (1 - 2 * side)
+
+                counts[side] = counts[side] + jnp.where(belongs, 1, 0)
+
             @pl.when(~mine)
-            def _(count=count):
-                list_ref[k, count] = w
-                list_ref[k, terms + count] = jnp.where(place < 0, place + blocks, place)
+            def _():
                 left_high[w, k], left_low[w, k] = left
                 right_high[w, k], right_low[w, k] = right
 
-            count = count + jnp.where(mine, 0, 1)
-        list_ref[k, 2 * terms] = count
-
-
-def other_kernel(
-    list_ref, after_ref, before_ref, left_high, left_low, right_high, right_low, sum_ref,
+        for side in (0, 1):
+            list_ref[k, side * 8 + 2 * terms] = counts[side]
+
+
+def side_kernel(
+    side, list_ref, received_ref, left_high, left_low, right_high, right_low, sum_ref,
     total_ref, high_ref, low_ref,
 ):
     terms, blocks, rows, columns = left_high.shape
-    parts, _, part, _ = total_ref.shape
-    for i in range(2 * blocks):
-        value = before_ref[i] if i < blocks else after_ref[i - blocks]
-        high_ref[i], low_ref[i] = split(value)
-    counts = [list_ref[k, 2 * terms] for k in range(blocks)]
+    parts = total_ref.shape[0]
+    base = side * 8
+    for i in range(blocks):
+        high_ref[i], low_ref[i] = split(received_ref[i])
+    counts = [list_ref[k, base + 2 * terms] for k in range(blocks)]
     both = functools.reduce(jnp.minimum, counts)
 
-    def first_product(k, j):
-        w = jnp.clip(list_ref[k, j], 0, terms - 1)
-        i = jnp.clip(list_ref[k, terms + j], 0, 2 * blocks - 1)
+    def term(k, j):
+        w = jnp.clip(list_ref[k, base + j], 0, terms - 1)
+        i = jnp.clip(list_ref[k, base + terms + j], 0, blocks - 1)
         done = product((left_high[w, k], left_low[w, k]), (high_ref[i], low_ref[i]), 0)
-        return split(done), (right_high[w, k], right_low[w, k])
-
-    def sum_of_terms(k, places):
-        pairs = [first_product(k, j) for j in places]
-        left, right = (
-            tuple(jnp.concatenate([pair[side][part] for pair in pairs], axis=1) for part in (0, 1))
-            for side in (0, 1)
-        )
-        return arranged(product(left, right, 1), parts)
-
-    @pl.when(both >= 2)
+        return arranged(product(split(done), (right_high[w, k], right_low[w, k]), 1), parts)
+
+    @pl.when(both >= 1)
     def _():
         for k in range(blocks):
-            total_ref[:, k] = sum_ref[:, k] + sum_of_terms(k, (0, 1))
-
-    @pl.when(both < 2)
+            total_ref[:, k] = sum_ref[:, k] + term(k, 0)
+
+    @pl.when(both < 1)
     def _():
         total_ref[...] = sum_ref[...]
         for k in range(blocks):
-            for j in range(min(2, terms)):
-
-                @pl.when(j < counts[k])
-                def _():
-                    total_ref[:, k] += sum_of_terms(k, (j,))
-
-    for j in range(2, terms):
+
+            @pl.when(counts[k] > 0)
+            def _():
+                total_ref[:, k] += term(k, 0)
+
+    for j in range(1, terms):
         for k in range(blocks):
 
             @pl.when(j < counts[k])
             def _():
-                total_ref[:, k] += sum_of_terms(k, (j,))
+                total_ref[:, k] += term(k, j)
 
 
 def on_device(wavefunction, sector_sizes, left_env, right_env, mpo_coeffs, source_block):
@@ -195,7 +193,7 @@
 
     total, *halves, others = pl.pallas_call(
         own_kernel,
-        out_shape=[share] + [half] * 4 + [jax.ShapeDtypeStruct((blocks, 8), jnp.int32)],
+        out_shape=[share] + [half] * 4 + [jax.ShapeDtypeStruct((blocks, 16), jnp.int32)],
         in_specs=[hbm] * 3 + [vmem] + [hbm] * 2,
         out_specs=[vmem] * 5 + [smem],
         scratch_shapes=[
@@ -212,16 +210,17 @@
         name="own_terms",
     )(sector_sizes, coeffs, sources, masked, left_env, right_env)
 
-    total = pl.pallas_call(
-        other_kernel,
-        out_shape=share,
-        in_specs=[smem] + [vmem] * 7,
-        out_specs=vmem,
-        scratch_shapes=[pltpu.VMEM((2 * blocks, rows, columns), jnp.bfloat16)] * 2,
-        compiler_params=params,
-        cost_estimate=cost,
-        name="other_terms",
-    )(others, after, before, *halves, total)
+    for side, received in enumerate((before, after)):
+        total = pl.pallas_call(
+            functools.partial(side_kernel, side),
+            out_shape=pltpu.VMEM(share.shape, jnp.float32),
+            in_specs=[smem] + [vmem] * 6,
+            out_specs=vmem,
+            scratch_shapes=[pltpu.VMEM((blocks, rows, columns), jnp.bfloat16)] * 2,
+            compiler_params=params,
+            cost_estimate=cost,
+            name=("before_terms", "after_terms")[side],
+        )(others, received, *halves, total)
 
     shares = lax.all_to_all(total, "mpo", split_axis=0, concat_axis=0, tiled=True, axis_index_groups=[order(parts)])
     return shares.sum(0)

time: 46 us -> 45.9 us (level)
  the two profiles are of different devices: /device:TPU:112 before, /device:TPU:1 now
where the time goes in v4:
time: 45.9 us; the launch traced here: 45.6 us
  blocking collectives  18.4 us (40%)
  starting transfers between devices  17.4 us (38%)
  Pallas kernels  7.69 us (17%)
  local copies, waits for them, and re-layouts  1.42 us (3%)
  other arithmetic  0.66 us (1%)
    all_to_all x1, blocking collectives, on_device(): lax.all_to_all(total, 'mpo', split_axis=0, concat_axis=0, tiled=True, axi...  18.4 us
    ppermute x1, starting transfers between devices, on_device(): after = lax.ppermute(masked, 'sec', down)  11.1 us
    ppermute x1, starting transfers between devices, on_device(): before = lax.ppermute(masked, 'sec', up)  6.3 us
    pallas_call x1, Pallas kernels, on_device(): pl.pallas_call(own_kernel, out_shape=[share] + [half] * 4 + [jax.ShapeDty...  3.57 us
    pallas_call x2, Pallas kernels, on_device(): pl.pallas_call(functools.partial(side_kernel, side), out_shape=pltpu.VMEM...  2.92 us
    unnamed x10, local copies, waits for them, and re-layouts  1.42 us
    pallas_call x1, Pallas kernels, on_device(): pl.pallas_call(mask_kernel, out_shape=pltpu.VMEM(wavefunction.shape, jnp....  1.2 us
  transfers between devices with their start and end apart: 2, of which 0 were waited for; matrix products, arithmetic and copies ran while one was open for 0% of the time, Pallas kernels for 11%

profile of v4, /device:TPU:1, one launch (start us, length us, event | category | flops | bytes accessed | tf_op | source)
XLA Modules:
  0.0 45.6 jit_solution(7067372944190193135)
XLA Ops:
  0.0 0.0 copy-start.2
  0.0 0.0 copy-start.3
  0.0 0.0 copy-start.4
  0.0 0.0 copy-start
  0.0 1.2 %mask.1.masked_ref = f32[2,256,256]{2,1,0:T(8,128)S(1)} custom-call(s32[2,2]{1,0:T(2,128)} %sizes_hbm.3, f32[2,256,256]{2,1,0:T(8,128)} %wave_hbm.1), custom_call_target="tpu_custom_call" | custom-call | flops 10000000000 | bytes 1 | tf_op jit(solution)/shard_map/mask/pallas_call | solution.py:176
  1.2 6.3 %collective-permute-start.1 = (f32[2,256,256]{2,1,0:T(8,128)S(1)}, f32[2,256,256]{2,1,0:T(8,128)S(1)}, u32[]{:S(2)}, u32[]{:S(2)}) collective-permute-start(f32[2,256,256]{2,1,0:T(8,128)S(1)} %mask.1.masked_ref), channel_id=1, source_target_pairs={{0,8},{8,16},{16,24},{24,32},{32,40},{40,48},{48,56},{56,64},{64,7... | collective-permute-start | bytes 1572872 | tf_op jit(solution)/shard_map/ppermute | solution.py:191
  7.5 11.1 %collective-permute-start = (f32[2,256,256]{2,1,0:T(8,128)S(1)}, f32[2,256,256]{2,1,0:T(8,128)S(1)}, u32[]{:S(2)}, u32[]{:S(2)}) collective-permute-start(f32[2,256,256]{2,1,0:T(8,128)S(1)} %mask.1.masked_ref), channel_id=1, source_target_pairs={{8,0},{16,8},{24,16},{32,24},{40,32},{48,40},{56,48},{64,56},{72,6... | collective-permute-start | bytes 1572872 | tf_op jit(solution)/shard_map/ppermute | solution.py:192
  18.6 0.0 copy-done.2
  18.6 0.0 copy-done.3
  18.6 0.0 copy-done.4
  18.6 0.0 copy-done
  18.7 0.0 copy-start.1
  18.7 1.4 %copy-done.1 = f32[3,2,256,256]{3,2,1,0:T(8,128)S(1)} copy-done((f32[3,2,256,256]{3,2,1,0:T(8,128)S(1)}, f32[3,2,256,256]{3,2,1,0:T(8,128)}, u32[]{:S(2)}) %copy-start.1) | copy-done | bytes 1572888
  20.1 3.6 %own_terms.1 = (f32[8,2,32,256]{3,2,1,0:T(8,128)S(1)}, bf16[3,2,256,256]{3,2,1,0:T(8,128)(2,1)S(1)}, bf16[3,2,256,256]{3,2,1,0:T(8,128)(2,1)S(1)}, bf16[3,2,256,...) custom-call(s32[2,2]{1,0:T(2,128)S(1)} %copy-done.2, f32[2,3]{1,0:T(2,128)S(1)} %bitcast.2, ...), custom_call_target="tpu_custom_call" | custom-call | flops 10000000000 | bytes 1 | tf_op jit(solution)/shard_map/own_terms/pallas_call | solution.py:194
  23.6 0.0 collective-permute-done.1.received_ref
  23.7 1.5 %before_terms.1.sum_ref = f32[8,2,32,256]{3,2,1,0:T(8,128)S(1)} custom-call(s32[2,16]{1,0:T(2,128)S(1)} %get-tuple-element.11.list_ref, f32[2,256,256]{2,1,0:T(8,128)S(1)} %collective-permute-done.1.received_ref, bf16[3,2,256,256]{3,2,1,0:T(8,128)(2,1)S(1)} %get-tuple-element.12.left_high, bf16[3,2,256,256]{3,2,1,0:T(8,128)(2,1)S(1)} %get-tuple-element.13.left_low, ...), custom_call_target="tpu_custom_call" | custom-call | flops 10000000000 | bytes 1 | tf_op jit(solution)/shard_map/before_terms/pallas_call | solution.py:214
  25.1 0.0 collective-permute-done.received_ref
  25.1 1.5 %after_terms.1 = f32[8,2,32,256]{3,2,1,0:T(8,128)S(1)} custom-call(s32[2,16]{1,0:T(2,128)S(1)} %get-tuple-element.11.list_ref, f32[2,256,256]{2,1,0:T(8,128)S(1)} %collective-permute-done.received_ref, bf16[3,2,256,256]{3,2,1,0:T(8,128)(2,1)S(1)} %get-tuple-element.12.left_high, bf16[3,2,256,256]{3,2,1,0:T(8,128)(2,1)S(1)} %get-tuple-element.13.left_low, ...), custom_call_target="tpu_custom_call" | custom-call | flops 10000000000 | bytes 1 | tf_op jit(solution)/shard_map/after_terms/pallas_call | solution.py:214
  26.6 18.4 %all_to_all.5 = f32[8,2,32,256]{3,2,1,0:T(8,128)S(1)} all-to-all(f32[8,2,32,256]{3,2,1,0:T(8,128)S(1)} %after_terms.1), channel_id=1, replica_groups={{4,3,2,1,0,7,6,5},{12,11,10,9,8,15,14,13},{20,19,18,17,16,23,22,21},{28..., dimensions={0} | all-to-all | bytes 1048576 | tf_op jit(solution)/shard_map/all_to_all | solution.py:225
  45.0 0.7 %reduce_sum.9 = f32[2,32,256]{2,1,0:T(8,128)} reduce(f32[8,2,32,256]{3,2,1,0:T(8,128)S(1)} %all_to_all.5, f32[]{:T(128)} %constant.0.clone.1), dimensions={0}, to_apply=%region_0.0 | reduce | flops 114688 | bytes 589828 | tf_op jit(solution)/shard_map/reduce_sum | solution.py:226
Async XLA Ops:
  0.0 18.6 %copy-start.2 = (s32[2,2]{1,0:T(2,128)S(1)}, s32[2,2]{1,0:T(2,128)}, u32[]{:S(2)}) copy-start(s32[2,2]{1,0:T(2,128)} %sizes_hbm.3) | copy-start | bytes 52
  0.0 18.6 %copy-start.3 = (f32[3,2]{0,1:T(2,128)S(1)}, f32[3,2]{0,1:T(2,128)}, u32[]{:S(2)}) copy-start(f32[3,2]{0,1:T(2,128)} %param.10) | copy-start | bytes 76
  0.0 18.6 %copy-start.4 = (s32[3,2]{0,1:T(2,128)S(1)}, s32[3,2]{0,1:T(2,128)}, u32[]{:S(2)}) copy-start(s32[3,2]{0,1:T(2,128)} %param.11) | copy-start | bytes 76
  0.0 18.6 %copy-start = (f32[3,2,256,256]{3,2,1,0:T(8,128)S(1)}, f32[3,2,256,256]{3,2,1,0:T(8,128)}, u32[]{:S(2)}) copy-start(f32[3,2,256,256]{3,2,1,0:T(8,128)} %left_hbm.1) | copy-start | bytes 4718596
  1.2 22.4 %collective-permute-start.1 = (f32[2,256,256]{2,1,0:T(8,128)S(1)}, f32[2,256,256]{2,1,0:T(8,128)S(1)}, u32[]{:S(2)}, u32[]{:S(2)}) collective-permute-start(f32[2,256,256]{2,1,0:T(8,128)S(1)} %mask.1.masked_ref), channel_id=1, source_target_pairs={{0,8},{8,16},{16,24},{24,32},{32,40},{40,48},{48,56},{56,64},{64,7... | collective-permute-start | bytes 1572872 | tf_op jit(solution)/shard_map/ppermute | solution.py:191
  7.5 17.6 %collective-permute-start = (f32[2,256,256]{2,1,0:T(8,128)S(1)}, f32[2,256,256]{2,1,0:T(8,128)S(1)}, u32[]{:S(2)}, u32[]{:S(2)}) collective-permute-start(f32[2,256,256]{2,1,0:T(8,128)S(1)} %mask.1.masked_ref), channel_id=1, source_target_pairs={{8,0},{16,8},{24,16},{32,24},{40,32},{48,40},{56,48},{64,56},{72,6... | collective-permute-start | bytes 1572872 | tf_op jit(solution)/shard_map/ppermute | solution.py:192
  18.7 1.4 %copy-start.1 = (f32[3,2,256,256]{3,2,1,0:T(8,128)S(1)}, f32[3,2,256,256]{3,2,1,0:T(8,128)}, u32[]{:S(2)}) copy-start(f32[3,2,256,256]{3,2,1,0:T(8,128)} %right_hbm.1) | copy-start | bytes 4718596
